TPU v7x, 32 devices: a whole 2x2x4 slice. The times are simulated.
32 devices in a mesh: rows: 8 (over z, x), rep: 4 (over y, core).
Axes of the slice: x: 2, y: 2, z: 4, core: 2. Of those that a mesh axis runs over, the one named last changes fastest.
Arguments:
- p_blocks: bfloat16 [64, 12, 128, 128], P('rows'), may hold values from -1.25 to 1.25
- d_blocks: bfloat16 [64, 12, 128, 128], P('rows'), may hold values from -1.25 to 1.25
- p_cols: int32 [64, 12], replicated, may hold values from 0 to 63, as said below
- d_cols: int32 [64, 12], replicated, may hold values from 0 to 63, as said below
- out_pcols: int32 [64, 12], P('rows'), may hold values from 0 to 63, as said below
- out_dcols: int32 [64, 12], P('rows'), may hold values from 0 to 63, as said below
- row_slot: int32 [64], replicated, may hold values from 0 to 63, as said below
- branch: int32 [64], P('rows'), may hold values from 0 to 1
Outputs:
- next_p: bfloat16 [64, 12, 128, 128], P('rows', 'rep')
- next_d: bfloat16 [64, 12, 128, 128], P('rows', 'rep')
Inputs may be any that keep to these rules, and one draw needn't show every extreme that they name: row_slot is a permutation; global block row g is stored at position row_slot[g], on index row_slot[g] // 8 of rows, and never more than 3 positions away from g. `p_cols`: the stored row s that holds global block row g names 12 different global block columns, g among them, each equal to (g + o) mod 64 with -12 <= o <= 12. `d_cols`: as for p_cols. `out_pcols`: as for p_cols. `out_dcols`: as for p_cols.
All inputs are finite; a program needn't handle non-finite values.
Results may differ from a plain program's by a relative error of at most 0.0095.
Values may be sent and summed in bfloat16 or wider, within the bound.
A program may use at most 192 MiB of HBM per device.

v0:
```python
import jax
import jax.numpy as jnp
from jax import lax
from jax.sharding import PartitionSpec as P


def shifted(value, axis, steps):
    count = lax.axis_size(axis)
    pairs = [(source, (source + steps) % count) for source in range(count)]
    return lax.ppermute(value, axis, pairs)


def local(p_blocks, d_blocks, p_cols, d_cols, out_pcols, out_dcols, row_slot, branch):
    slab_rows = p_blocks.shape[0]
    slot_count = p_blocks.shape[1]
    block_side = p_blocks.shape[2]
    quarter = slot_count // lax.axis_size("rep")
    all_rows = slab_rows * lax.axis_size("rows")
    row_start = lax.axis_index("rows") * slab_rows
    slot_start = lax.axis_index("rep") * quarter
    margin_rows = slab_rows + slot_count - 2
    reach_dev = (slab_rows + margin_rows - 1) // slab_rows
    p_part = lax.dynamic_slice_in_dim(p_blocks, slot_start, quarter, 1)
    d_part = lax.dynamic_slice_in_dim(d_blocks, slot_start, quarter, 1)
    ordered = []
    for distance in range(-reach_dev, reach_dev + 1):
        if distance == 0:
            ordered.append((p_part, d_part))
            continue
        if distance < 0:
            first_row = max(0, -distance * slab_rows - margin_rows)
            last_row = slab_rows
        else:
            first_row = 0
            last_row = min(slab_rows, margin_rows - (distance - 1) * slab_rows)
        ordered.append(
            shifted((p_part[first_row:last_row], d_part[first_row:last_row]), "rows", -distance)
        )
    cand_p = jnp.concatenate([received_slab[0] for received_slab in ordered], axis=0)
    cand_d = jnp.concatenate([received_slab[1] for received_slab in ordered], axis=0)
    own_pcols = lax.dynamic_slice_in_dim(p_cols, row_start, slab_rows, 0)
    own_dcols = lax.dynamic_slice_in_dim(d_cols, row_start, slab_rows, 0)
    right_pcols = lax.dynamic_slice_in_dim(p_cols, slot_start, quarter, 1)
    right_dcols = lax.dynamic_slice_in_dim(d_cols, slot_start, quarter, 1)
    slot_range = jnp.arange(slot_count, dtype=jnp.int32)
    row_range = jnp.arange(slab_rows, dtype=jnp.int32)

    def block_product(pairs, out_ids):
        total = jnp.zeros((slab_rows * (slot_count + 1), block_side, block_side), jnp.float32)
        for left_blocks, left_ids, right_blocks, right_ids_all in pairs:
            stored = jnp.take(row_slot, left_ids, axis=0)
            located = (stored - row_start + margin_rows) % all_rows
            right_rows = jnp.take(right_blocks, located, axis=0)
            right_ids = jnp.take(right_ids_all, stored, axis=0)
            matches = right_ids[:, :, :, None] == out_ids[:, None, None, :]
            found = jnp.any(matches, axis=3)
            target = jnp.sum(jnp.where(matches, slot_range[None, None, None, :], 0), axis=3)
            target = jnp.where(found, target, slot_count)
            flat_target = (row_range[:, None, None] * (slot_count + 1) + target).reshape(-1)
            block_terms = jnp.einsum(
                "skab,skmbc->skmac", left_blocks, right_rows, preferred_element_type=jnp.float32
            )
            total = total.at[flat_target].add(block_terms.reshape(-1, block_side, block_side))
        return total.reshape(slab_rows, slot_count + 1, block_side, block_side)[:, :slot_count]

    square = block_product([(p_blocks, own_pcols, cand_p, right_pcols)], out_pcols)
    tangent = block_product(
        [(p_blocks, own_pcols, cand_d, right_dcols), (d_blocks, own_dcols, cand_p, right_pcols)],
        out_dcols,
    )
    square, tangent = (
        lax.psum_scatter(
            square.astype(jnp.bfloat16), "rep", scatter_dimension=1, tiled=True
        ).astype(jnp.float32),
        lax.psum_scatter(
            tangent.astype(jnp.bfloat16), "rep", scatter_dimension=1, tiled=True
        ).astype(jnp.float32),
    )

    def kept_blocks(row_blocks, row_ids, out_ids):
        matches = row_ids[:, :, None] == out_ids[:, None, :]
        position = jnp.sum(jnp.where(matches, slot_range[None, :, None], 0), axis=1)
        present = jnp.any(matches, axis=1)
        picked = jnp.take_along_axis(row_blocks, position[:, :, None, None], axis=1).astype(
            jnp.float32
        )
        return jnp.where(present[:, :, None, None], picked, 0.0)

    out_pquarter = lax.dynamic_slice_in_dim(out_pcols, slot_start, quarter, 1)
    out_dquarter = lax.dynamic_slice_in_dim(out_dcols, slot_start, quarter, 1)
    squaring = (branch == 1)[:, None, None, None]
    next_p = jnp.where(
        squaring, square, 2.0 * kept_blocks(p_blocks, own_pcols, out_pquarter) - square
    ).astype(jnp.bfloat16)
    next_d = jnp.where(
        squaring, tangent, 2.0 * kept_blocks(d_blocks, own_dcols, out_dquarter) - tangent
    ).astype(jnp.bfloat16)
    return (next_p, next_d)


def solution(mesh):
    return jax.shard_map(
        local,
        mesh=mesh,
        in_specs=(
            P("rows", None, None, None),
            P("rows", None, None, None),
            P(),
            P(),
            P("rows", None),
            P("rows", None),
            P(),
            P("rows"),
        ),
        out_specs=(P("rows", "rep", None, None), P("rows", "rep", None, None)),
        check_vma=False,
    )
```

profile of v0, /device:TPU:0, one launch (start us, length us, event | category | flops | bytes accessed | tf_op | source)
XLA Modules:
  0.0 643.9 jit_solution(16595290093848680057)
XLA Ops:
  35.6 43.8 %collective-permute-done.6 = bf16[2,3,128,128]{3,2,1,0:T(8,128)(2,1)S(1)} collective-permute-done((bf16[2,3,128,128]{3,2,1,0:T(8,128)(2,1)}, bf16[2,3,128,128]{3,2,1,0:T(8,128)(2,1)S(1)}, u32[]{:S(2)}, u32[]{:S(2)}) %collective-permute-start.6) | collective-permute-done | bytes 196640 | tf_op jit(solution)/shard_map/ppermute | solution.py:10
  80.1 25.0 %collective-permute-done = bf16[2,3,128,128]{3,2,1,0:T(8,128)(2,1)S(1)} collective-permute-done((bf16[2,3,128,128]{3,2,1,0:T(8,128)(2,1)}, bf16[2,3,128,128]{3,2,1,0:T(8,128)(2,1)S(1)}, u32[]{:S(2)}, u32[]{:S(2)}) %collective-permute-start) | collective-permute-done | bytes 196640 | tf_op jit(solution)/shard_map/ppermute | solution.py:10
  107.9 4.7 collective-permute-start.3
  123.1 22.3 %collective-permute-done.11 = bf16[2,3,128,128]{3,2,1,0:T(8,128)(2,1)S(1)} collective-permute-done((bf16[2,3,128,128]{3,2,1,0:T(8,128)(2,1)S(1)}, bf16[2,3,128,128]{3,2,1,0:T(8,128)(2,1)S(1)}, u32[]{:S(2)}, u32[]{:S(2)}) %collective-permute-start.11) | collective-permute-done | bytes 196640 | tf_op jit(solution)/shard_map/ppermute | solution.py:10
  145.4 4.3 collective-permute-start.5
  150.4 9.9 %gather_fusion.5 = bf16[96,3,128,128]{3,2,1,0:T(8,128)(2,1)} fusion(bf16[44,3,128,128]{3,2,1,0:T(8,128)(2,1)} %constant_dynamic-update-slice_fusion.7, s32[1024]{0:T(1024)S(1)} %pad_clamp_fusion.3), kind=kCustom, calls=%fused_computation.7.clone | custom fusion | bytes 18874752 | tf_op jit(solution)/shard_map/jit(_take)/gather | solution.py:53
  160.3 12.7 %copy.107 = bf16[8,12,3,128,128]{3,4,2,1,0:T(8,128)(2,1)} copy(bf16[8,12,3,128,128]{4,3,2,1,0:T(8,128)(2,1)} %bitcast.74) | data formatting | bytes 18874368 | tf_op jit(solution)/shard_map/jit(_take)/gather | solution.py:53
  173.0 10.2 %fusion.2 = f32[8,12,3,128,128]{4,3,2,1,0:T(8,128)} fusion(bf16[8,12,3,128,128]{3,4,2,1,0:T(8,128)(2,1)} %copy.107, pred[8,12]{1,0:T(8,128)(4,1)S(1)} %get-tuple-element.16, bf16[8,12,128,128]{3,2,1,0:T(8,128)(2,1)S(1)} %copy-done.2), kind=kOutput, calls=%fused_computation.15 | convolution fusion | flops 1212678144 | bytes 31457376 | tf_op jit(solution)/shard_map/skab,skmbc->skmac/dot_general | solution.py:60
  190.4 18.6 %copy.108 = f32[288,128,128]{2,1,0:T(8,128)} copy(f32[288,128,128]{1,2,0:T(8,128)} %bitcast.69) | data formatting | bytes 37748736 | tf_op jit(solution)/shard_map/reshape | solution.py:63
  211.9 9.7 %gather_fusion.2 = bf16[96,3,128,128]{3,2,1,0:T(8,128)(2,1)} fusion(bf16[44,3,128,128]{3,2,1,0:T(8,128)(2,1)} %constant_dynamic-update-slice_fusion, s32[1024]{0:T(1024)S(1)} %pad_clamp_fusion.3), kind=kCustom, calls=%fused_computation.2.clone | custom fusion | bytes 18874752 | tf_op jit(solution)/shard_map/jit(_take)/gather | solution.py:53
  221.6 9.8 %gather_fusion.8 = bf16[96,3,128,128]{3,2,1,0:T(8,128)(2,1)} fusion(bf16[44,3,128,128]{3,2,1,0:T(8,128)(2,1)} %constant_dynamic-update-slice_fusion, s32[1024]{0:T(1024)S(1)} %pad_clamp_fusion), kind=kCustom, calls=%fused_computation.8.clone | custom fusion | bytes 18874752 | tf_op jit(solution)/shard_map/jit(_take)/gather | solution.py:53
  231.4 12.7 %copy.115 = bf16[8,12,3,128,128]{3,4,2,1,0:T(8,128)(2,1)} copy(bf16[8,12,3,128,128]{4,3,2,1,0:T(8,128)(2,1)} %bitcast.73) | data formatting | bytes 18874368 | tf_op jit(solution)/shard_map/jit(_take)/gather | solution.py:53
  244.1 11.9 %fusion = f32[8,12,3,128,128]{4,3,2,1,0:T(8,128)} fusion(bf16[8,12,3,128,128]{3,4,2,1,0:T(8,128)(2,1)} %copy.115, pred[8,12]{1,0:T(8,128)(4,1)S(1)} %get-tuple-element.12, bf16[8,12,128,128]{3,2,1,0:T(8,128)(2,1)} %param.17), kind=kOutput, calls=%fused_computation.13 | convolution fusion | flops 1212678144 | bytes 31457376 | tf_op jit(solution)/shard_map/skab,skmbc->skmac/dot_general | solution.py:60
  256.0 18.7 %copy.116 = f32[288,128,128]{2,1,0:T(8,128)} copy(f32[288,128,128]{1,2,0:T(8,128)} %bitcast.70) | data formatting | bytes 37748736 | tf_op jit(solution)/shard_map/reshape | solution.py:63
  278.3 58.4 %scatter_fusion.1 = f32[104,128,128]{2,1,0:T(8,128)} fusion(f32[104,128,128]{2,1,0:T(8,128)} %broadcast.150.clone.1, s32[288]{0:T(512)S(1)} %fusion.25, f32[288,128,128]{2,1,0:T(8,128)} %copy.108), kind=kCustom, calls=%fused_computation.11 | custom fusion | flops 4718592 | bytes 56624256 | tf_op jit(solution)/shard_map/scatter-add | solution.py:63
  336.7 58.2 %scatter_fusion.2 = f32[104,128,128]{2,1,0:T(8,128)} fusion(f32[104,128,128]{2,1,0:T(8,128)} %scatter_fusion.1, s32[288]{0:T(512)S(1)} %fusion.26, f32[288,128,128]{2,1,0:T(8,128)} %copy.116), kind=kCustom, calls=%fused_computation.12 | custom fusion | flops 4718592 | bytes 56624256 | tf_op jit(solution)/shard_map/scatter-add | solution.py:63
  395.0 3.7 convert.9
  400.5 12.7 %copy.95 = bf16[8,12,3,128,128]{3,4,2,1,0:T(8,128)(2,1)} copy(bf16[8,12,3,128,128]{4,3,2,1,0:T(8,128)(2,1)} %bitcast.72) | data formatting | bytes 18874368 | tf_op jit(solution)/shard_map/jit(_take)/gather | solution.py:53
  413.2 10.2 %fusion.4 = f32[8,12,3,128,128]{4,3,2,1,0:T(8,128)} fusion(bf16[8,12,3,128,128]{3,4,2,1,0:T(8,128)(2,1)} %copy.95, pred[8,12]{1,0:T(8,128)(4,1)S(1)} %get-tuple-element.16, bf16[8,12,128,128]{3,2,1,0:T(8,128)(2,1)S(1)} %copy-done.2), kind=kOutput, calls=%fused_computation.17 | convolution fusion | flops 1212678144 | bytes 31457376 | tf_op jit(solution)/shard_map/skab,skmbc->skmac/dot_general | solution.py:60
  423.4 18.6 %copy.96 = f32[288,128,128]{2,1,0:T(8,128)} copy(f32[288,128,128]{1,2,0:T(8,128)} %bitcast.71) | data formatting | bytes 37748736 | tf_op jit(solution)/shard_map/reshape | solution.py:63
  445.7 58.8 %scatter_fusion = f32[104,128,128]{2,1,0:T(8,128)} fusion(f32[104,128,128]{2,1,0:T(8,128)} %broadcast.150.clone, s32[288]{0:T(512)S(1)} %fusion.24, f32[288,128,128]{2,1,0:T(8,128)} %copy.96), kind=kCustom, calls=%fused_computation.10 | custom fusion | flops 4718592 | bytes 56624256 | tf_op jit(solution)/shard_map/scatter-add | solution.py:63
  504.5 3.7 convert.8
  519.2 113.9 %all-reduce.5.cloned.1.call-done = (bf16[8,12,128,128]{3,2,1,0:T(8,128)(2,1)}, bf16[8,12,128,128]{3,2,1,0:T(8,128)(2,1)}) async-done(((bf16[8,12,128,128]{3,2,1,0:T(8,128)(2,1)}, bf16[8,12,128,128]{3,2,1,0:T(8,128)(2,1)}), (bf16[8,12,128,128]{3,2,1,0:T(8,128)(2,1)}, bf16[8,12,128,128]{3,2,1,0:T(8,128)(2,1)})) %all-reduce.5.cloned.1.call-update) | async-done | bytes 6291472
  633.2 3.9 fusion.16
  (156 shorter events, 72.3 us)
Async XLA Ops:
  7.2 14.5 %copy-start = (s32[64]{0:T(128)S(1)}, s32[64]{0:T(128)}, u32[]{:S(2)}) copy-start(s32[64]{0:T(128)} %param.22) | copy-start | bytes 772
  7.2 626.0 %all-reduce.5.cloned.1.call-start = ((), (), s32[]{:S(2)}) async-start(), calls=%async_computation | async-start | bytes 12582912
  9.3 96.5 %collective-permute-start.7 = (bf16[8,3,128,128]{3,2,1,0:T(8,128)(2,1)}, bf16[8,3,128,128]{3,2,1,0:T(8,128)(2,1)}, u32[]{:S(2)}, u32[]{:S(2)}) collective-permute-start(bf16[8,3,128,128]{3,2,1,0:T(8,128)(2,1)} %constant_dynamic-slice_fusion.4), channel_id=1, source_target_pairs={{0,8},{4,12},{8,16},{12,20},{16,24},{20,28},{24,0},{28,4},{1,9},{5... | collective-permute-start | bytes 2359304 | tf_op jit(solution)/shard_map/ppermute | solution.py:10
  12.4 95.5 %collective-permute-start.8 = (bf16[8,3,128,128]{3,2,1,0:T(8,128)(2,1)}, bf16[8,3,128,128]{3,2,1,0:T(8,128)(2,1)}, u32[]{:S(2)}, u32[]{:S(2)}) collective-permute-start(bf16[8,3,128,128]{3,2,1,0:T(8,128)(2,1)} %constant_dynamic-slice_fusion.4), channel_id=1, source_target_pairs={{0,4},{4,8},{8,12},{12,16},{16,20},{20,24},{24,28},{28,0},{1,5},{5... | collective-permute-start | bytes 2359304 | tf_op jit(solution)/shard_map/ppermute | solution.py:10
  13.8 102.9 %collective-permute-start.9 = (bf16[8,3,128,128]{3,2,1,0:T(8,128)(2,1)}, bf16[8,3,128,128]{3,2,1,0:T(8,128)(2,1)}, u32[]{:S(2)}, u32[]{:S(2)}) collective-permute-start(bf16[8,3,128,128]{3,2,1,0:T(8,128)(2,1)} %constant_dynamic-slice_fusion.4), channel_id=1, source_target_pairs={{0,28},{4,0},{8,4},{12,8},{16,12},{20,16},{24,20},{28,24},{1,29},{... | collective-permute-start | bytes 2359304 | tf_op jit(solution)/shard_map/ppermute | solution.py:10
  17.1 102.4 %collective-permute-start.10 = (bf16[8,3,128,128]{3,2,1,0:T(8,128)(2,1)}, bf16[8,3,128,128]{3,2,1,0:T(8,128)(2,1)}, u32[]{:S(2)}, u32[]{:S(2)}) collective-permute-start(bf16[8,3,128,128]{3,2,1,0:T(8,128)(2,1)} %constant_dynamic-slice_fusion.4), channel_id=1, source_target_pairs={{0,24},{4,28},{8,0},{12,4},{16,8},{20,12},{24,16},{28,20},{1,25},{... | collective-permute-start | bytes 2359304 | tf_op jit(solution)/shard_map/ppermute | solution.py:10
  19.1 60.3 %collective-permute-start.6 = (bf16[2,3,128,128]{3,2,1,0:T(8,128)(2,1)}, bf16[2,3,128,128]{3,2,1,0:T(8,128)(2,1)S(1)}, u32[]{:S(2)}, u32[]{:S(2)}) collective-permute-start(bf16[2,3,128,128]{3,2,1,0:T(8,128)(2,1)} %get-tuple-element.21), channel_id=1, source_target_pairs={{0,12},{4,16},{8,20},{12,24},{16,28},{20,0},{24,4},{28,8},{1,13},{... | collective-permute-start | bytes 589832 | tf_op jit(solution)/shard_map/ppermute | solution.py:10
  21.5 1.7 copy-start.4
  21.6 4.9 copy-start.6
  21.7 5.8 copy-start.8
  22.9 7.5 %copy-start.10 = (s32[8,12]{1,0:T(8,128)S(1)}, s32[8,12]{1,0:T(8,128)}, u32[]{:S(2)}) copy-start(s32[8,12]{1,0:T(8,128)} %param.20) | copy-start | bytes 1156
  22.9 9.1 %copy-start.2 = (bf16[8,12,128,128]{3,2,1,0:T(8,128)(2,1)S(1)}, bf16[8,12,128,128]{3,2,1,0:T(8,128)(2,1)}, u32[]{:S(2)}) copy-start(bf16[8,12,128,128]{3,2,1,0:T(8,128)(2,1)} %param.16) | copy-start | bytes 9437188
  35.6 81.2 %copy-start.3 = (bf16[2,3,128,128]{3,2,1,0:T(8,128)(2,1)S(1)}, bf16[2,3,128,128]{3,2,1,0:T(8,128)(2,1)}, u32[]{:S(2)}) copy-start(bf16[2,3,128,128]{3,2,1,0:T(8,128)(2,1)} %get-tuple-element.20) | copy-start | bytes 589828
  79.4 25.7 %collective-permute-start = (bf16[2,3,128,128]{3,2,1,0:T(8,128)(2,1)}, bf16[2,3,128,128]{3,2,1,0:T(8,128)(2,1)S(1)}, u32[]{:S(2)}, u32[]{:S(2)}) collective-permute-start(bf16[2,3,128,128]{3,2,1,0:T(8,128)(2,1)} %get-tuple-element.23), channel_id=1, source_target_pairs={{0,12},{4,16},{8,20},{12,24},{16,28},{20,0},{24,4},{28,8},{1,13},{... | collective-permute-start | bytes 589832 | tf_op jit(solution)/shard_map/ppermute | solution.py:10
  105.1 78.2 %collective-permute-start.1 = (bf16[8,3,128,128]{3,2,1,0:T(8,128)(2,1)}, bf16[8,3,128,128]{3,2,1,0:T(8,128)(2,1)}, u32[]{:S(2)}, u32[]{:S(2)}) collective-permute-start(bf16[8,3,128,128]{3,2,1,0:T(8,128)(2,1)} %constant_dynamic-slice_fusion.8), channel_id=1, source_target_pairs={{0,8},{4,12},{8,16},{12,20},{16,24},{20,28},{24,0},{28,4},{1,9},{5... | collective-permute-start | bytes 2359304 | tf_op jit(solution)/shard_map/ppermute | solution.py:10
  105.8 79.5 %collective-permute-start.2 = (bf16[8,3,128,128]{3,2,1,0:T(8,128)(2,1)}, bf16[8,3,128,128]{3,2,1,0:T(8,128)(2,1)}, u32[]{:S(2)}, u32[]{:S(2)}) collective-permute-start(bf16[8,3,128,128]{3,2,1,0:T(8,128)(2,1)} %constant_dynamic-slice_fusion.8), channel_id=1, source_target_pairs={{0,4},{4,8},{8,12},{12,16},{16,20},{20,24},{24,28},{28,0},{1,5},{5... | collective-permute-start | bytes 2359304 | tf_op jit(solution)/shard_map/ppermute | solution.py:10
  107.9 80.5 %collective-permute-start.3 = (bf16[8,3,128,128]{3,2,1,0:T(8,128)(2,1)}, bf16[8,3,128,128]{3,2,1,0:T(8,128)(2,1)}, u32[]{:S(2)}, u32[]{:S(2)}) collective-permute-start(bf16[8,3,128,128]{3,2,1,0:T(8,128)(2,1)} %constant_dynamic-slice_fusion.8), channel_id=1, source_target_pairs={{0,28},{4,0},{8,4},{12,8},{16,12},{20,16},{24,20},{28,24},{1,29},{... | collective-permute-start | bytes 2359304 | tf_op jit(solution)/shard_map/ppermute | solution.py:10
  116.8 28.6 %collective-permute-start.11 = (bf16[2,3,128,128]{3,2,1,0:T(8,128)(2,1)S(1)}, bf16[2,3,128,128]{3,2,1,0:T(8,128)(2,1)S(1)}, u32[]{:S(2)}, u32[]{:S(2)}) collective-permute-start(bf16[2,3,128,128]{3,2,1,0:T(8,128)(2,1)S(1)} %copy-done.3), channel_id=1, source_target_pairs={{0,20},{4,24},{8,28},{12,0},{16,4},{20,8},{24,12},{28,16},{1,21},{... | collective-permute-start | bytes 589832 | tf_op jit(solution)/shard_map/ppermute | solution.py:10
  119.5 89.6 %collective-permute-start.4 = (bf16[8,3,128,128]{3,2,1,0:T(8,128)(2,1)}, bf16[8,3,128,128]{3,2,1,0:T(8,128)(2,1)}, u32[]{:S(2)}, u32[]{:S(2)}) collective-permute-start(bf16[8,3,128,128]{3,2,1,0:T(8,128)(2,1)} %constant_dynamic-slice_fusion.8), channel_id=1, source_target_pairs={{0,24},{4,28},{8,0},{12,4},{16,8},{20,12},{24,16},{28,20},{1,25},{... | collective-permute-start | bytes 2359304 | tf_op jit(solution)/shard_map/ppermute | solution.py:10
  145.4 65.8 %collective-permute-start.5 = (bf16[2,3,128,128]{3,2,1,0:T(8,128)(2,1)}, bf16[2,3,128,128]{3,2,1,0:T(8,128)(2,1)S(1)}, u32[]{:S(2)}, u32[]{:S(2)}) collective-permute-start(bf16[2,3,128,128]{3,2,1,0:T(8,128)(2,1)} %get-tuple-element.22), channel_id=1, source_target_pairs={{0,20},{4,24},{8,28},{12,0},{16,4},{20,8},{24,12},{28,16},{1,21},{... | collective-permute-start | bytes 589832 | tf_op jit(solution)/shard_map/ppermute | solution.py:10
  510.1 1.2 copy-start.7
  510.2 7.8 %copy-start.13 = (u32[32]{0:T(128)S(1)}, u32[32]{0:T(128)}, u32[]{:S(2)}) copy-start(u32[32]{0:T(128)} %constant.135) | copy-start | bytes 388
  510.2 9.0 %copy-start.12 = (s32[8]{0:T(128)S(1)}, s32[8]{0:T(128)}, u32[]{:S(2)}) copy-start(s32[8]{0:T(128)} %param.23) | copy-start | bytes 100
  510.2 126.9 %copy-start.1 = (s32[64]{0:T(128)S(1)}, s32[64]{0:T(128)}, u32[]{:S(2)}) copy-start(s32[64]{0:T(128)} %param.22) | copy-start | bytes 772
  (3 other events, 2.5 us)
Sparse Core Ops, SparseCore 0:
  510.3 122.7 all-reduce.4
where the time goes:
time: 648 us; the launch traced here: 644 us
  waiting for transfers between devices  205 us (32%)
  other arithmetic  192 us (30%)
  local copies, waits for them, and re-layouts  180 us (28%)
  matrix products  32.4 us (5%)
  starting transfers between devices  19.1 us (3%)
  between operations  15 us (2%)
    scatter-add x3, other arithmetic, block_product(): total.at[flat_target].add(block_terms.reshape(-1, block_side, block_side))  175 us
    unnamed x2, waiting for transfers between devices  114 us
    ppermute x12, waiting for transfers between devices, shifted(): return lax.ppermute(value, axis, pairs)  91.1 us
    gather x6, local copies, waits for them, and re-layouts, block_product(): right_rows = jnp.take(right_blocks, located, axis=0)  67.5 us
    reshape x3, local copies, waits for them, and re-layouts, block_product(): block_terms.reshape(-1, block_side, block_side)  56 us
    dot_general x3, matrix products, block_product(): jnp.einsum('skab,skmbc->skmac', left_blocks, right_rows, preferred_elemen...  32.4 us
    unnamed x45, local copies, waits for them, and re-layouts  22.9 us
    ppermute x12, starting transfers between devices, shifted(): return lax.ppermute(value, axis, pairs)  19.1 us
  transfers between devices with their start and end apart: 13, of which 4 were waited for; matrix products, arithmetic and copies ran while one was open for 15% of the time, Pallas kernels for 0%

commit v1 on v0

v1 whole, which is shorter than its diff:
```python
import functools

import jax
import jax.numpy as jnp
from jax import lax
from jax.experimental import pallas as pl
from jax.experimental.pallas import tpu as pltpu
from jax.sharding import PartitionSpec as P

MESH = pl.DeviceIdType.MESH
MOVE = 3


def nt_dot(left, right):
    return lax.dot_general(
        left, right, (((1,), (1,)), ((), ())), preferred_element_type=jnp.float32
    )


def pack_kernel(pick_ref, p_ref, d_ref, out_ref):
    slots, side = p_ref.shape[1], p_ref.shape[2]
    width = pick_ref.shape[0]
    for which, ref in enumerate((p_ref, d_ref)):
        cut = nt_dot(pick_ref[...], ref[0].reshape(slots * side, side)).astype(jnp.bfloat16)
        for m in range(slots):
            out_ref[0, which, m * width : (m + 1) * width, :] = cut[:, m * side : (m + 1) * side]


def pack(pick, p_blocks, d_blocks):
    rows, slots, side, _ = p_blocks.shape
    width = pick.shape[0]
    block = pl.BlockSpec((1, slots, side, side), lambda s: (s, 0, 0, 0))
    return pl.pallas_call(
        pack_kernel,
        grid=(rows,),
        in_specs=[pl.BlockSpec((width, side), lambda s: (0, 0)), block, block],
        out_specs=pl.BlockSpec((1, 2, slots * width, side), lambda s: (s, 0, 0, 0)),
        out_shape=jax.ShapeDtypeStruct((rows, 2, slots * width, side), jnp.bfloat16),
    )(pick, p_blocks, d_blocks)


def gather_kernel(count, chunks, base, own_ref, cand_ref, send_sem, recv_sem, local_sem):
    me = lax.axis_index("rows")
    parity = lax.rem(me, 2)
    sign = 1 - 2 * parity

    def at(distance):
        return lax.rem(me + distance + 4 * count, count)

    partner, far, back, edge_dev = at(sign), at(2 * sign), at(-2 * sign), at(-3 * sign)
    barrier = pltpu.get_barrier_semaphore()
    for other in (partner, far, back, edge_dev):
        pl.semaphore_signal(barrier, inc=1, device_id={"rows": other}, device_id_type=MESH)
    pl.semaphore_wait(barrier, 4)

    def copy(src, place, sem, device):
        return pltpu.make_async_remote_copy(
            src_ref=src,
            dst_ref=cand_ref.at[place],
            send_sem=send_sem.at[sem],
            recv_sem=recv_sem.at[sem],
            device_id={"rows": device},
            device_id_type=MESH,
        )

    def slot(distance, chunk):
        return base + distance * chunks + chunk

    to_back = [copy(own_ref.at[c], slot(2 * sign, c), c, back) for c in range(chunks)]
    to_partner = [copy(own_ref.at[c], slot(-sign, c), chunks + c, partner) for c in range(chunks)]
    to_far = [copy(own_ref.at[c], slot(-2 * sign, c), 2 * chunks + c, far) for c in range(chunks)]
    first = parity * (chunks - 1)
    last = (1 - parity) * (chunks - 1)
    edge = copy(own_ref.at[first], slot(3 * sign, first), 4 * chunks, edge_dev)
    stay = pltpu.make_async_copy(own_ref, cand_ref.at[pl.ds(base, chunks)], local_sem)
    for c in range(chunks):
        to_back[c].start()
        to_far[c].start()
        to_partner[c].start()
    edge.start()
    stay.start()

    def arrived(distance, chunk, sem):
        place = slot(distance, chunk)
        copy(cand_ref.at[place], place, sem, partner).wait_recv()

    onward = []
    for c in range(chunks):
        arrived(2 * sign, c, c)
        passed = copy(cand_ref.at[slot(2 * sign, c)], slot(sign, c), 3 * chunks + c, partner)
        passed.start()
        onward.append(passed)
    arrived(-2 * sign, last, 2 * chunks + last)
    passed = copy(
        cand_ref.at[slot(-2 * sign, last)], slot(-3 * sign, last), 4 * chunks + 1, partner
    )
    passed.start()
    onward.append(passed)

    for c in range(chunks):
        arrived(sign, c, chunks + c)
    for i in range(1, chunks):
        rest = lax.rem(last + i, chunks)
        arrived(-2 * sign, rest, 2 * chunks + rest)
    for c in range(chunks):
        arrived(-sign, c, 3 * chunks + c)
    arrived(-3 * sign, last, 4 * chunks)
    arrived(3 * sign, first, 4 * chunks + 1)
    for sent in (*to_back, *to_partner, *to_far, edge, *onward):
        sent.wait_send()
    stay.wait()


def gather(packed, count, margin):
    rows = packed.shape[0]
    chunk = margin - 2 * rows
    chunks, base = rows // chunk, margin // chunk
    tail = packed.shape[1:]
    places = 2 * base + chunks
    out = pl.pallas_call(
        functools.partial(gather_kernel, count, chunks, base),
        in_specs=[pl.BlockSpec(memory_space=pl.ANY)],
        out_specs=pl.BlockSpec(memory_space=pl.ANY),
        out_shape=jax.ShapeDtypeStruct((places, chunk, *tail), packed.dtype),
        scratch_shapes=[
            pltpu.SemaphoreType.DMA((4 * chunks + 2,)),
            pltpu.SemaphoreType.DMA((4 * chunks + 2,)),
            pltpu.SemaphoreType.DMA,
        ],
        compiler_params=pltpu.CompilerParams(collective_id=0, has_side_effects=True),
    )(packed.reshape(chunks, chunk, *tail))
    return out.reshape(places * chunk, *tail)


def multiply_kernel(table_ref, p_ref, d_ref, cand_ref, out_ref, right, left):
    slots, side = p_ref.shape[1], p_ref.shape[2]
    reps, _, _, quarter, width, _ = out_ref.shape
    s = pl.program_id(0)
    sums = []
    for pairs in ((0,), (1, 2)):
        total = None
        for pair in pairs:
            lref = d_ref if pair == 2 else p_ref
            for k in range(slots):
                left[:, k * side : (k + 1) * side] = lref[0, k]
                for j in range(slots):
                    place = table_ref[pair, s, k, j]
                    right[pair, j * width : (j + 1) * width, k * side : (k + 1) * side] = cand_ref[
                        place
                    ]
            part = nt_dot(right[pair], left[...])
            total = part if total is None else total + part
        sums.append(total)
    for which, total in enumerate(sums):
        out_ref[:, 0, which] = total.astype(jnp.bfloat16).reshape(reps, quarter, width, side)


def multiply(table, p_blocks, d_blocks, cand, reps):
    rows, slots, side, _ = p_blocks.shape
    width = cand.shape[1]
    quarter = slots // reps
    block = pl.BlockSpec((1, slots, side, side), lambda s, t: (s, 0, 0, 0))
    return pl.pallas_call(
        multiply_kernel,
        grid_spec=pltpu.PrefetchScalarGridSpec(
            num_scalar_prefetch=1,
            grid=(rows,),
            in_specs=[block, block, pl.BlockSpec(memory_space=pltpu.VMEM)],
            out_specs=pl.BlockSpec(
                (reps, 1, 2, quarter, width, side), lambda s, t: (0, s, 0, 0, 0, 0)
            ),
            scratch_shapes=[
                pltpu.VMEM((3, slots * width, slots * side), jnp.bfloat16),
                pltpu.VMEM((side, slots * side), jnp.bfloat16),
            ],
        ),
        out_shape=jax.ShapeDtypeStruct((reps, rows, 2, quarter, width, side), jnp.bfloat16),
        compiler_params=pltpu.CompilerParams(vmem_limit_bytes=48 * 1024 * 1024),
    )(table, p_blocks, d_blocks, cand)


def finish_kernel(keep_ref, bit_ref, eye_ref, sum_ref, p_ref, d_ref, outp_ref, outd_ref):
    quarter, side = outp_ref.shape[1], outp_ref.shape[2]
    slots = p_ref.shape[1]
    s = pl.program_id(0)
    squaring = bit_ref[s] == 1
    for which, (ref, out) in enumerate(((p_ref, outp_ref), (d_ref, outd_ref))):
        for j in range(quarter):
            total = nt_dot(eye_ref[...], sum_ref[:, 0, which, j].reshape(side, side))
            place = keep_ref[which, s, j]
            kept = ref[0, jnp.minimum(place, slots - 1)].astype(jnp.float32)
            kept = jnp.where(place < slots, kept, 0.0)
            out[0, j] = jnp.where(squaring, total, 2.0 * kept - total).astype(jnp.bfloat16)


def finish(keep, bits, eye, sums, p_blocks, d_blocks):
    rows, slots, side, _ = p_blocks.shape
    reps, _, _, quarter, width, _ = sums.shape
    block = pl.BlockSpec((1, slots, side, side), lambda s, k, b: (s, 0, 0, 0))
    out = pl.BlockSpec((1, quarter, side, side), lambda s, k, b: (s, 0, 0, 0))
    shape = jax.ShapeDtypeStruct((rows, quarter, side, side), jnp.bfloat16)
    return pl.pallas_call(
        finish_kernel,
        grid_spec=pltpu.PrefetchScalarGridSpec(
            num_scalar_prefetch=2,
            grid=(rows,),
            in_specs=[
                pl.BlockSpec((side, side), lambda s, k, b: (0, 0)),
                pl.BlockSpec((reps, 1, 2, quarter, width, side), lambda s, k, b: (0, s, 0, 0, 0, 0)),
                block,
                block,
            ],
            out_specs=[out, out],
        ),
        out_shape=[shape, shape],
    )(keep, bits, eye, sums, p_blocks, d_blocks)


def local(p_blocks, d_blocks, p_cols, d_cols, out_pcols, out_dcols, row_slot, branch):
    rows, slots, side = p_blocks.shape[:3]
    reps, count = lax.axis_size("rep"), lax.axis_size("rows")
    quarter, width = slots // reps, side // reps
    all_rows = rows * count
    margin = slots + 2 * MOVE
    row_start = lax.axis_index("rows") * rows
    rep = lax.axis_index("rep")

    pick = (
        jnp.arange(width, dtype=jnp.int32)[:, None] + rep * width
        == jnp.arange(side, dtype=jnp.int32)[None, :]
    ).astype(jnp.bfloat16)
    packed = pack(pick, p_blocks, d_blocks)
    cand = gather(packed, count, margin)
    cand_rows = cand.shape[0]
    blocks = cand.reshape(cand_rows * 2 * slots, width, side)
    nothing = cand_rows * 2 * slots
    blocks = jnp.concatenate([blocks, jnp.zeros((1, width, side), blocks.dtype)], axis=0)

    own_p = lax.dynamic_slice_in_dim(p_cols, row_start, rows, 0)
    own_d = lax.dynamic_slice_in_dim(d_cols, row_start, rows, 0)
    every = jnp.arange(all_rows, dtype=jnp.int32)
    slot_range = jnp.arange(slots, dtype=jnp.int32)

    def locate(ids):
        stored = jnp.sum(jnp.where(ids[:, :, None] == every, row_slot, 0), axis=2)
        return stored, (stored - row_start + margin) % all_rows

    stored_p, near_p = locate(own_p)
    stored_d, near_d = locate(own_d)

    def entries(stored, near, right_cols, which, out_ids):
        right = jnp.sum(
            jnp.where((stored[:, :, None] == every)[..., None], right_cols, 0), axis=2
        )
        matches = right[:, :, :, None] == out_ids[:, None, None, :]
        m = jnp.sum(jnp.where(matches, slot_range[:, None] + 1, 0), axis=2)
        return jnp.where(m > 0, (near[:, :, None] * 2 + which) * slots + m - 1, nothing)

    table = jnp.stack(
        [
            entries(stored_p, near_p, p_cols, 0, out_pcols),
            entries(stored_p, near_p, d_cols, 1, out_dcols),
            entries(stored_d, near_d, p_cols, 0, out_dcols),
        ]
    ).astype(jnp.int32)

    def positions(ids, out_ids):
        out_ids = lax.dynamic_slice_in_dim(out_ids, rep * quarter, quarter, 1)
        matches = ids[:, :, None] == out_ids[:, None, :]
        found = jnp.sum(jnp.where(matches, slot_range[:, None] + 1, 0), axis=1)
        return jnp.where(found > 0, found - 1, slots)

    keep = jnp.stack([positions(own_p, out_pcols), positions(own_d, out_dcols)]).astype(jnp.int32)
    parts = multiply(table, p_blocks, d_blocks, blocks, reps)
    sums = lax.all_to_all(parts, "rep", 0, 0)
    eye = jnp.eye(side, dtype=jnp.bfloat16)
    next_p, next_d = finish(keep, branch, eye, sums, p_blocks, d_blocks)
    return next_p, next_d


def solution(mesh):
    return jax.shard_map(
        local,
        mesh=mesh,
        in_specs=(
            P("rows", None, None, None),
            P("rows", None, None, None),
            P(),
            P(),
            P("rows", None),
            P("rows", None),
            P(),
            P("rows"),
        ),
        out_specs=(P("rows", "rep", None, None), P("rows", "rep", None, None)),
        check_vma=False,
    )
```

time: 648 us -> 177 us (0.27)
  waiting for transfers between devices: 205 us -> 18 us
  other arithmetic: 192 us -> 11.9 us
  local copies, waits for them, and re-layouts: 180 us -> 11.4 us
  Pallas kernels: 0 us -> 130 us
  matrix products: 32.4 us -> 0 us
  starting transfers between devices: 19.1 us -> 3.56 us
  between operations: 15 us -> 0.8 us
    scatter-add x3 -> x0, other arithmetic: 175 us -> none  [block_product(): total.at[flat_target].add(block_terms.reshape(-1, block_side, block_side))]
    pallas_call x0 -> x4, Pallas kernels: none -> 130 us  [the longest x1 94.8 us: gather(): pl.pallas_call(functools.partial(gather_kernel, count, chunks, base), in_...]
    unnamed x2 -> x0, waiting for transfers between devices: 114 us -> none
    ppermute x12 -> x0, waiting for transfers between devices: 91.1 us -> none  [shifted(): return lax.ppermute(value, axis, pairs)]
    gather x25 -> x0, local copies, waits for them, and re-layouts: 77.9 us -> none  [the longest x6 67.5 us: block_product(): right_rows = jnp.take(right_blocks, located, axis=0)]
    reshape x3 -> x0, local copies, waits for them, and re-layouts: 56 us -> none  [block_product(): block_terms.reshape(-1, block_side, block_side)]
    dot_general x3 -> x0, matrix products: 32.4 us -> none  [block_product(): jnp.einsum('skab,skmbc->skmac', left_blocks, right_rows, preferred_elemen...]
    unnamed x45 -> x12, local copies, waits for them, and re-layouts: 22.9 us -> 1.18 us
  transfers between devices with their start and end apart: 13 -> 1, of which waited for: 4 -> 1; matrix products, arithmetic and copies ran while one was open for 15% -> 1% of each run, Pallas kernels for 0% -> 0%
where the time goes in v1:
time: 177 us; the launch traced here: 176 us
  Pallas kernels  130 us (73%)
  waiting for transfers between devices  18 us (10%)
  other arithmetic  11.9 us (7%)
  local copies, waits for them, and re-layouts  11.4 us (6%)
  starting transfers between devices  3.56 us (2%)
    pallas_call x1, Pallas kernels, gather(): pl.pallas_call(functools.partial(gather_kernel, count, chunks, base), in_...  94.8 us
    pallas_call x1, Pallas kernels, multiply(): pl.pallas_call(multiply_kernel, grid_spec=pltpu.PrefetchScalarGridSpec(nu...  19.7 us
    all_to_all x1, waiting for transfers between devices, local(): sums = lax.all_to_all(parts, 'rep', 0, 0)  18 us
    pallas_call x1, Pallas kernels, finish(): pl.pallas_call(finish_kernel, grid_spec=pltpu.PrefetchScalarGridSpec(num_...  8.22 us
    concatenate x1, local copies, waits for them, and re-layouts, local(): jnp.concatenate([blocks, jnp.zeros((1, width, side), blocks.dtype)], axis=0)  7.93 us
    pallas_call x1, Pallas kernels, pack(): pl.pallas_call(pack_kernel, grid=(rows,), in_specs=[pl.BlockSpec((width,...  7.63 us
    reduce_sum x1, other arithmetic, entries(): jnp.sum(jnp.where((stored[:, :, None] == every)[..., None], right_cols, 0...  7.35 us
    all_to_all x1, starting transfers between devices, local(): sums = lax.all_to_all(parts, 'rep', 0, 0)  3.56 us
  transfers between devices with their start and end apart: 1, of which 1 were waited for; matrix products, arithmetic and copies ran while one was open for 1% of the time, Pallas kernels for 0%

profile of v1, /device:TPU:0, one launch (start us, length us, event | category | flops | bytes accessed | tf_op | source)
XLA Modules:
  0.0 175.9 jit_solution(16439203628623784674)
XLA Ops:
  0.6 0.8 constant_dynamic-slice_fusion.1
  1.4 0.8 constant_dynamic-slice_fusion.3
  2.2 1.2 select_reduce_fusion.7
  3.5 0.1 iota_compare_fusion.1
  3.7 0.7 fusion.7.pick_ref
  4.3 7.6 %shard_map.95 = bf16[8,2,384,128]{3,2,1,0:T(8,128)(2,1)} custom-call(bf16[32,128]{1,0:T(8,128)(2,1)} %fusion.7.pick_ref, bf16[8,12,128,128]{3,2,1,0:T(8,128)(2,1)} %p_ref.5, bf16[8,12,128,128]{3,2,1,0:T(8,128)(2,1)} %d_ref.5), custom_call_target="tpu_custom_call" | custom-call | tf_op jit(solution)/shard_map/pallas_call | solution.py:33
  12.0 94.8 %shard_map.96 = bf16[22,2,2,384,128]{4,3,2,1,0:T(8,128)(2,1)} custom-call(bf16[4,2,2,384,128]{4,3,2,1,0:T(8,128)(2,1)} %bitcast.34), custom_call_target="tpu_custom_call" | custom-call | tf_op jit(solution)/shard_map/pallas_call | solution.py:120
  106.8 7.4 %select_reduce_fusion.5 = (s32[8,12,12]{0,2,1:T(8,128)S(1)}, s32[8,12,12]{0,2,1:T(8,128)S(1)}, s32[8,12,12]{0,2,1:T(8,128)S(1)}) fusion(s32[64,12]{0,1:T(8,128)S(1)} %copy-done.2, pred[8,12,64]{2,0,1:T(8,128)(4,1)S(1)} %get-tuple-element.18, s32[64,12]{0,1:T(8,128)S(1)} %copy-done.3, pred[8,12,64]{2,0,1:T(8,128)(4,1)S(1)} %get-tuple-element.17), kind=kLoop, calls=%fused_computation.5 | loop fusion | flops 438912 | bytes 32256 | tf_op jit(solution)/shard_map/reduce_sum | solution.py:252
  114.2 0.8 select_reduce_fusion.2
  115.0 0.1 fusion.5
  115.1 0.1 fusion.3
  115.2 0.1 fusion.1
  115.3 7.9 %concatenate.3.cand_ref = bf16[1057,32,128]{2,1,0:T(8,128)(2,1)} pad(bf16[1056,32,128]{2,1,0:T(8,128)(2,1)} %bitcast.33, bf16[]{:T(256)} %constant.62.clone.1), padding=0_1x0_0x0_0 | pad | bytes 17309698 | tf_op jit(solution)/shard_map/concatenate | solution.py:237
  123.3 19.7 %shard_map.97 = bf16[4,8,2,3,32,128]{5,4,3,2,1,0:T(8,128)(2,1)} custom-call(s32[3,8,12,12]{3,2,1,0:T(8,128)S(1)} %pad_add_fusion.table_ref, bf16[8,12,128,128]{3,2,1,0:T(8,128)(2,1)S(1)} %copy-done, bf16[8,12,128,128]{3,2,1,0:T(8,128)(2,1)} %d_ref.5, bf16[1057,32,128]{2,1,0:T(8,128)(2,1)} %concatenate.3.cand_ref), custom_call_target="tpu_custom_call" | custom-call | tf_op jit(solution)/shard_map/pallas_call | solution.py:163
  142.9 3.6 %all-to-all-start = ((bf16[4,8,2,3,32,128]{5,4,3,2,1,0:T(8,128)(2,1)}), bf16[4,8,2,3,32,128]{5,4,3,2,1,0:T(8,128)(2,1)S(1)}, u32[]{:S(2)}, u32[]{:S(2)}) async-start(bf16[4,8,2,3,32,128]{5,4,3,2,1,0:T(8,128)(2,1)} %shard_map.97), calls=%async_computation | async-start | bytes 3145728 | tf_op jit(solution)/shard_map/all_to_all | solution.py:275
  146.7 0.1 copy.40
  146.9 0.2 select_reduce_fusion.9
  147.2 0.1 copy.43
  147.3 0.1 copy.44
  147.3 0.6 pad_add_fusion.1.keep_ref
  147.9 0.6 fusion.6.eye_ref
  148.6 18.0 %all-to-all-done.sum_ref = bf16[4,8,2,3,32,128]{5,4,3,2,1,0:T(8,128)(2,1)S(1)} async-done(((bf16[4,8,2,3,32,128]{5,4,3,2,1,0:T(8,128)(2,1)}), bf16[4,8,2,3,32,128]{5,4,3,2,1,0:T(8,128)(2,1)S(1)}, u32[]{:S(2)}, u32[]{:S(2)}) %all-to-all-start) | async-done | bytes 1572896 | tf_op jit(solution)/shard_map/all_to_all | solution.py:275
  166.6 1.2 copy-done.1
  167.7 8.2 %shard_map.98 = (bf16[8,3,128,128]{3,2,1,0:T(8,128)(2,1)}, bf16[8,3,128,128]{3,2,1,0:T(8,128)(2,1)}) custom-call(s32[2,8,3]{2,1,0:T(8,128)} %pad_add_fusion.1.keep_ref, s32[8]{0:T(128)} %bit_ref.1, bf16[128,128]{1,0:T(8,128)(2,1)} %fusion.6.eye_ref, bf16[4,8,2,3,32,128]{5,4,3,2,1,0:T(8,128)(2,1)} %copy-done.1, bf16[8,12,128,128]{3,2,1,0:T(8,128)(2,1)} %p_ref.5, ...), custom_call_target="tpu_custom_call" | custom-call | tf_op jit(solution)/shard_map/pallas_call | solution.py:202
  (23 shorter events, 0.5 us)
Async XLA Ops:
  12.0 94.8 %copy-start.2 = (s32[64,12]{0,1:T(8,128)S(1)}, s32[64,12]{0,1:T(8,128)}, u32[]{:S(2)}) copy-start(s32[64,12]{0,1:T(8,128)} %param.10) | copy-start | bytes 9220
  12.0 94.8 %copy-start.3 = (s32[64,12]{0,1:T(8,128)S(1)}, s32[64,12]{0,1:T(8,128)}, u32[]{:S(2)}) copy-start(s32[64,12]{0,1:T(8,128)} %param.11) | copy-start | bytes 9220
  12.0 102.2 %copy-start.4 = (s32[8,12]{1,0:T(8,128)S(1)}, s32[8,12]{1,0:T(8,128)}, u32[]{:S(2)}) copy-start(s32[8,12]{1,0:T(8,128)} %param.13) | copy-start | bytes 1156
  12.0 102.2 %copy-start.5 = (s32[8,12]{1,0:T(8,128)S(1)}, s32[8,12]{1,0:T(8,128)}, u32[]{:S(2)}) copy-start(s32[8,12]{1,0:T(8,128)} %param.12) | copy-start | bytes 1156
  115.3 8.0 %copy-start = (bf16[8,12,128,128]{3,2,1,0:T(8,128)(2,1)S(1)}, bf16[8,12,128,128]{3,2,1,0:T(8,128)(2,1)}, u32[]{:S(2)}) copy-start(bf16[8,12,128,128]{3,2,1,0:T(8,128)(2,1)} %p_ref.5) | copy-start | bytes 9437188
  142.9 23.6 %all-to-all-start = ((bf16[4,8,2,3,32,128]{5,4,3,2,1,0:T(8,128)(2,1)}), bf16[4,8,2,3,32,128]{5,4,3,2,1,0:T(8,128)(2,1)S(1)}, u32[]{:S(2)}, u32[]{:S(2)}) async-start(bf16[4,8,2,3,32,128]{5,4,3,2,1,0:T(8,128)(2,1)} %shard_map.97), calls=%async_computation | async-start | bytes 3145728 | tf_op jit(solution)/shard_map/all_to_all | solution.py:275
  166.6 1.2 copy-start.1
